TPU v7x, 32 devices: a whole 2x2x4 slice. The times are simulated.
32 devices in a mesh: parts: 2 (over y), blk: 16 (over z, x, core).
Axes of the slice: x: 2, y: 2, z: 4, core: 2. Of those that a mesh axis runs over, the one named last changes fastest.
Arguments:
- emb: bfloat16 [4096, 1024], P(('parts', 'blk')), parts along dimension 0, may hold values from -11 to 11
- cluster: int32 [4096], P(('parts', 'blk')), parts along dimension 0, may hold values from 0 to 3, as said below
Outputs:
- neighbour_mean: bfloat16 [4096, 1024], P(('parts', 'blk')), parts along dimension 0
- dup_score: float32 [4096], P(('parts', 'blk')), parts along dimension 0
There are 2 independent parts, one for each index of `parts`. A program takes and returns all parts, laid end to end along the dimension named above; each array names one. Nothing has to cross between parts.
Inputs may be any that keep to these rules, and one draw needn't show every extreme that they name: `cluster`: clusters r * 4 to r * 4 + 3 form group r. Among the rows of one device (aligned blocks of 128 rows) at most 128 lie in one group's clusters; in every draw one group has exactly 128 rows on every device.
All inputs are finite; a program needn't handle non-finite values.
Results may differ from a plain program's by a relative error of at most 0.0022.
Values may be sent and summed in bfloat16 or wider, within the bound.
A program may use at most 64 MiB of HBM per device.

v0:
```python
import jax
import jax.numpy as jnp
from jax import lax
from jax.sharding import PartitionSpec as P

CYCLE = 16
CL_CYCLE = 4


SHARPNESS = 2.0


def passed_along(block, axis, distance):
    devices = range(lax.axis_size(axis))
    route = [((i - distance) % len(devices), i) for i in devices]
    return lax.ppermute(block, axis, route)


def squares(rows):
    return jnp.sum(jnp.square(rows.astype(jnp.float32)), 1)


def weights(home_rows, home_norm, home_ids, visit_rows, visit_ids, skip_self):
    visit_norm = squares(visit_rows)
    inner = lax.dot_general(
        home_rows, visit_rows, (((1,), (1,)), ((), ())), preferred_element_type=jnp.float32
    )
    distance = jnp.maximum(home_norm[:, None] + visit_norm[None, :] - 2.0 * inner, 0.0)
    allowed = (home_ids[:, None] == visit_ids[None, :]) & (home_ids[:, None] >= 0)
    if skip_self:
        row_pos = jnp.arange(home_rows.shape[0], dtype=jnp.int32)
        allowed = allowed & (row_pos[:, None] != row_pos[None, :])
    return jnp.where(allowed, jnp.exp(-SHARPNESS * distance / home_rows.shape[1]), 0.0)


def absorb(weight, visit_rows, pulled, totals):
    pulled = pulled + jnp.dot(
        weight.astype(jnp.bfloat16), visit_rows, preferred_element_type=jnp.float32
    )
    return (pulled, totals + jnp.sum(weight, 1))


def local(emb, cluster):
    devices = lax.axis_size("blk")
    groups = devices // CYCLE
    doc_rows, width = emb.shape
    capacity = min(doc_rows // CYCLE, 3 * doc_rows // (2 * CYCLE * groups))
    slots = devices * capacity
    group_of = cluster // CL_CYCLE
    member = (group_of[:, None] == jnp.arange(groups, dtype=jnp.int32)[None, :]).astype(jnp.int32)
    running = jnp.cumsum(member, 0) - member
    place = jnp.sum(running * member, 1)
    target = place % CYCLE * groups + group_of
    slot_index = target * capacity + place // CYCLE
    send_rows = jnp.zeros((slots, width), jnp.bfloat16).at[slot_index].set(emb)
    send_ids = jnp.full((slots,), -1, jnp.int32).at[slot_index].set(cluster)
    got_rows, got_ids = (
        lax.all_to_all(
            send_rows.reshape(devices, capacity, width),
            "blk",
            split_axis=0,
            concat_axis=0,
            tiled=True,
        ),
        lax.all_to_all(
            send_ids.reshape(devices, capacity), "blk", split_axis=0, concat_axis=0, tiled=True
        ),
    )
    home_rows = got_rows.reshape(slots, width)
    home_ids = got_ids.reshape(slots)
    home_norm = squares(home_rows)
    pulled = jnp.zeros((slots, width), jnp.float32)
    totals = jnp.zeros((slots,), jnp.float32)
    weight = weights(home_rows, home_norm, home_ids, home_rows, home_ids, True)
    pulled, totals = absorb(weight, home_rows, pulled, totals)

    def advance(step, carry):
        visit_rows, visit_ids, pulled, totals = carry
        visit_rows, visit_ids = passed_along((visit_rows, visit_ids), "blk", groups)
        weight = weights(home_rows, home_norm, home_ids, visit_rows, visit_ids, False)
        pulled, totals = absorb(weight, visit_rows, pulled, totals)
        return (visit_rows, visit_ids, pulled, totals)

    _, _, pulled, totals = lax.fori_loop(1, CYCLE, advance, (home_rows, home_ids, pulled, totals))
    back_pulled, back_totals = (
        lax.all_to_all(
            pulled.reshape(devices, capacity, width), "blk", split_axis=0, concat_axis=0, tiled=True
        ),
        lax.all_to_all(
            totals.reshape(devices, capacity), "blk", split_axis=0, concat_axis=0, tiled=True
        ),
    )
    own_pulled = back_pulled.reshape(slots, width)[slot_index]
    own_totals = back_totals.reshape(slots)[slot_index]
    neighbour_mean = (own_pulled / (1.0 + own_totals)[:, None]).astype(jnp.bfloat16)
    dup_score = jnp.log(1.0 + own_totals)
    return (neighbour_mean, dup_score)


def solution(mesh):
    return jax.shard_map(
        local,
        mesh=mesh,
        in_specs=(P(("parts", "blk"), None), P(("parts", "blk"))),
        out_specs=(P(("parts", "blk"), None), P(("parts", "blk"))),
        check_vma=False,
    )
```

profile of v0, /device:TPU:1, one launch (start us, length us, event | category | flops | bytes accessed | tf_op | source)
XLA Modules:
  0.0 228.1 jit_solution(8304883580534434653)
XLA Ops:
  3.4 7.3 %all-to-all-start.1 = ((s32[16,1,8]{2,1,0:T(1,128)}), s32[16,1,8]{2,1,0:T(1,128)S(1)}, u32[]{:S(2)}, u32[]{:S(2)}) async-start(s32[16,1,8]{2,1,0:T(1,128)} %bitcast.3), calls=%async_computation.1 | async-start | bytes 16384 | tf_op jit(solution)/shard_map/all_to_all | solution.py:65
  12.9 3.6 %all-to-all-done.1 = s32[16,1,8]{2,1,0:T(1,128)S(1)} async-done(((s32[16,1,8]{2,1,0:T(1,128)}), s32[16,1,8]{2,1,0:T(1,128)S(1)}, u32[]{:S(2)}, u32[]{:S(2)}) %all-to-all-start.1) | async-done | bytes 544 | tf_op jit(solution)/shard_map/all_to_all | solution.py:65
  16.5 4.0 %all-to-all-start = ((bf16[16,8,1024]{2,1,0:T(8,128)(2,1)}), bf16[16,8,1024]{2,1,0:T(8,128)(2,1)S(1)}, u32[]{:S(2)}, u32[]{:S(2)}) async-start(bf16[16,8,1024]{2,1,0:T(8,128)(2,1)} %bitcast.1), calls=%async_computation | async-start | bytes 524288 | tf_op jit(solution)/shard_map/all_to_all | solution.py:58
  22.1 8.0 %all-to-all-done = bf16[16,8,1024]{2,1,0:T(8,128)(2,1)S(1)} async-done(((bf16[16,8,1024]{2,1,0:T(8,128)(2,1)}), bf16[16,8,1024]{2,1,0:T(8,128)(2,1)S(1)}, u32[]{:S(2)}, u32[]{:S(2)}) %all-to-all-start) | async-done | bytes 262176 | tf_op jit(solution)/shard_map/all_to_all | solution.py:58
  31.6 160.8 %while.19 = (s32[]{:T(128)}, bf16[128,1024]{1,0:T(8,128)(2,1)S(1)}, s32[128]{0:T(128)S(1)}, f32[128,1024]{1,0:T(8,128)}, f32[128]{0:T(128)S(1)}, /*index=5*/s32[...) while((s32[]{:T(128)}, bf16[128,1024]{1,0:T(8,128)(2,1)S(1)}, ...), condition=%wide.wide.region_8.9_spmd, body=%wide.wide.region_5.8_spmd.sunk | while | flops 67911680 | bytes 3811893 | solution.py:84
  32.4 2.6 %collective-permute-done.1 = s32[128]{0:T(128)S(1)} collective-permute-done((s32[128]{0:T(128)S(1)}, s32[128]{0:T(128)S(1)}, u32[]{:S(2)}, u32[]{:S(2)}) %collective-permute-start.1) | collective-permute-done | bytes 544 | tf_op jit(solution)/shard_map/while/body/eval_jaxpr/ppermute | solution.py:16
  37.6 2.5 %collective-permute-start = (bf16[128,1024]{1,0:T(8,128)(2,1)S(1)}, bf16[128,1024]{1,0:T(8,128)(2,1)S(1)}, u32[]{:S(2)}, u32[]{:S(2)}) collective-permute-start(bf16[128,1024]{1,0:T(8,128)(2,1)S(1)} %get-tuple-element.260), channel_id=1, source_target_pairs={{15,0},{0,1},{1,2},{2,3},{3,4},{4,5},{5,6},{6,7},{7,8},{8,9},{9,10... | collective-permute-start | bytes 786440 | tf_op jit(solution)/shard_map/while/body/eval_jaxpr/ppermute | solution.py:16
  40.2 4.4 %collective-permute-done.1 = s32[128]{0:T(128)S(1)} collective-permute-done((s32[128]{0:T(128)S(1)}, s32[128]{0:T(128)S(1)}, u32[]{:S(2)}, u32[]{:S(2)}) %collective-permute-start.1) | collective-permute-done | bytes 544 | tf_op jit(solution)/shard_map/while/body/eval_jaxpr/ppermute | solution.py:16
  48.6 7.1 %collective-permute-done.1 = s32[128]{0:T(128)S(1)} collective-permute-done((s32[128]{0:T(128)S(1)}, s32[128]{0:T(128)S(1)}, u32[]{:S(2)}, u32[]{:S(2)}) %collective-permute-start.1) | collective-permute-done | bytes 544 | tf_op jit(solution)/shard_map/while/body/eval_jaxpr/ppermute | solution.py:16
  58.3 8.5 %collective-permute-done.1 = s32[128]{0:T(128)S(1)} collective-permute-done((s32[128]{0:T(128)S(1)}, s32[128]{0:T(128)S(1)}, u32[]{:S(2)}, u32[]{:S(2)}) %collective-permute-start.1) | collective-permute-done | bytes 544 | tf_op jit(solution)/shard_map/while/body/eval_jaxpr/ppermute | solution.py:16
  69.5 8.5 %collective-permute-done.1 = s32[128]{0:T(128)S(1)} collective-permute-done((s32[128]{0:T(128)S(1)}, s32[128]{0:T(128)S(1)}, u32[]{:S(2)}, u32[]{:S(2)}) %collective-permute-start.1) | collective-permute-done | bytes 544 | tf_op jit(solution)/shard_map/while/body/eval_jaxpr/ppermute | solution.py:16
  80.7 8.5 %collective-permute-done.1 = s32[128]{0:T(128)S(1)} collective-permute-done((s32[128]{0:T(128)S(1)}, s32[128]{0:T(128)S(1)}, u32[]{:S(2)}, u32[]{:S(2)}) %collective-permute-start.1) | collective-permute-done | bytes 544 | tf_op jit(solution)/shard_map/while/body/eval_jaxpr/ppermute | solution.py:16
  91.8 8.5 %collective-permute-done.1 = s32[128]{0:T(128)S(1)} collective-permute-done((s32[128]{0:T(128)S(1)}, s32[128]{0:T(128)S(1)}, u32[]{:S(2)}, u32[]{:S(2)}) %collective-permute-start.1) | collective-permute-done | bytes 544 | tf_op jit(solution)/shard_map/while/body/eval_jaxpr/ppermute | solution.py:16
  103.0 8.5 %collective-permute-done.1 = s32[128]{0:T(128)S(1)} collective-permute-done((s32[128]{0:T(128)S(1)}, s32[128]{0:T(128)S(1)}, u32[]{:S(2)}, u32[]{:S(2)}) %collective-permute-start.1) | collective-permute-done | bytes 544 | tf_op jit(solution)/shard_map/while/body/eval_jaxpr/ppermute | solution.py:16
  114.2 8.5 %collective-permute-done.1 = s32[128]{0:T(128)S(1)} collective-permute-done((s32[128]{0:T(128)S(1)}, s32[128]{0:T(128)S(1)}, u32[]{:S(2)}, u32[]{:S(2)}) %collective-permute-start.1) | collective-permute-done | bytes 544 | tf_op jit(solution)/shard_map/while/body/eval_jaxpr/ppermute | solution.py:16
  125.4 8.5 %collective-permute-done.1 = s32[128]{0:T(128)S(1)} collective-permute-done((s32[128]{0:T(128)S(1)}, s32[128]{0:T(128)S(1)}, u32[]{:S(2)}, u32[]{:S(2)}) %collective-permute-start.1) | collective-permute-done | bytes 544 | tf_op jit(solution)/shard_map/while/body/eval_jaxpr/ppermute | solution.py:16
  136.5 8.5 %collective-permute-done.1 = s32[128]{0:T(128)S(1)} collective-permute-done((s32[128]{0:T(128)S(1)}, s32[128]{0:T(128)S(1)}, u32[]{:S(2)}, u32[]{:S(2)}) %collective-permute-start.1) | collective-permute-done | bytes 544 | tf_op jit(solution)/shard_map/while/body/eval_jaxpr/ppermute | solution.py:16
  147.7 8.5 %collective-permute-done.1 = s32[128]{0:T(128)S(1)} collective-permute-done((s32[128]{0:T(128)S(1)}, s32[128]{0:T(128)S(1)}, u32[]{:S(2)}, u32[]{:S(2)}) %collective-permute-start.1) | collective-permute-done | bytes 544 | tf_op jit(solution)/shard_map/while/body/eval_jaxpr/ppermute | solution.py:16
  158.9 8.5 %collective-permute-done.1 = s32[128]{0:T(128)S(1)} collective-permute-done((s32[128]{0:T(128)S(1)}, s32[128]{0:T(128)S(1)}, u32[]{:S(2)}, u32[]{:S(2)}) %collective-permute-start.1) | collective-permute-done | bytes 544 | tf_op jit(solution)/shard_map/while/body/eval_jaxpr/ppermute | solution.py:16
  170.1 8.5 %collective-permute-done.1 = s32[128]{0:T(128)S(1)} collective-permute-done((s32[128]{0:T(128)S(1)}, s32[128]{0:T(128)S(1)}, u32[]{:S(2)}, u32[]{:S(2)}) %collective-permute-start.1) | collective-permute-done | bytes 544 | tf_op jit(solution)/shard_map/while/body/eval_jaxpr/ppermute | solution.py:16
  181.2 8.5 %collective-permute-done.1 = s32[128]{0:T(128)S(1)} collective-permute-done((s32[128]{0:T(128)S(1)}, s32[128]{0:T(128)S(1)}, u32[]{:S(2)}, u32[]{:S(2)}) %collective-permute-start.1) | collective-permute-done | bytes 544 | tf_op jit(solution)/shard_map/while/body/eval_jaxpr/ppermute | solution.py:16
  192.5 15.8 %all_to_all.31 = f32[16,1,8]{2,1,0:T(1,128)S(1)} all-to-all(f32[16,1,8]{2,1,0:T(1,128)S(1)} %bitcast.33), channel_id=1, replica_groups=mesh['parts'=2,'blk'=16] {'blk'}, dimensions={0} | all-to-all | bytes 1024 | tf_op jit(solution)/shard_map/all_to_all | solution.py:89
  208.3 4.1 %all-to-all-start.2 = ((f32[16,8,1024]{2,1,0:T(8,128)}), f32[16,8,1024]{2,1,0:T(8,128)S(1)}, u32[]{:S(2)}, u32[]{:S(2)}) async-start(f32[16,8,1024]{2,1,0:T(8,128)} %bitcast.5), calls=%async_computation.2 | async-start | bytes 1048576 | tf_op jit(solution)/shard_map/all_to_all | solution.py:86
  215.4 11.1 %all-to-all-done.2 = f32[16,8,1024]{2,1,0:T(8,128)S(1)} async-done(((f32[16,8,1024]{2,1,0:T(8,128)}), f32[16,8,1024]{2,1,0:T(8,128)S(1)}, u32[]{:S(2)}, u32[]{:S(2)}) %all-to-all-start.2) | async-done | bytes 524320 | tf_op jit(solution)/shard_map/all_to_all | solution.py:86
  (180 shorter events, 54.2 us)
Async XLA Ops:
  3.4 13.1 %all-to-all-start.1 = ((s32[16,1,8]{2,1,0:T(1,128)}), s32[16,1,8]{2,1,0:T(1,128)S(1)}, u32[]{:S(2)}, u32[]{:S(2)}) async-start(s32[16,1,8]{2,1,0:T(1,128)} %bitcast.3), calls=%async_computation.1 | async-start | bytes 16384 | tf_op jit(solution)/shard_map/all_to_all | solution.py:65
  16.5 13.6 %all-to-all-start = ((bf16[16,8,1024]{2,1,0:T(8,128)(2,1)}), bf16[16,8,1024]{2,1,0:T(8,128)(2,1)S(1)}, u32[]{:S(2)}, u32[]{:S(2)}) async-start(bf16[16,8,1024]{2,1,0:T(8,128)(2,1)} %bitcast.1), calls=%async_computation | async-start | bytes 524288 | tf_op jit(solution)/shard_map/all_to_all | solution.py:58
  58.3 8.6 %collective-permute-start = (bf16[128,1024]{1,0:T(8,128)(2,1)S(1)}, bf16[128,1024]{1,0:T(8,128)(2,1)S(1)}, u32[]{:S(2)}, u32[]{:S(2)}) collective-permute-start(bf16[128,1024]{1,0:T(8,128)(2,1)S(1)} %get-tuple-element.260), channel_id=1, source_target_pairs={{15,0},{0,1},{1,2},{2,3},{3,4},{4,5},{5,6},{6,7},{7,8},{8,9},{9,10... | collective-permute-start | bytes 786440 | tf_op jit(solution)/shard_map/while/body/eval_jaxpr/ppermute | solution.py:16
  58.3 8.6 %collective-permute-start.1 = (s32[128]{0:T(128)S(1)}, s32[128]{0:T(128)S(1)}, u32[]{:S(2)}, u32[]{:S(2)}) collective-permute-start(s32[128]{0:T(128)S(1)} %get-tuple-element.261), channel_id=1, source_target_pairs={{15,0},{0,1},{1,2},{2,3},{3,4},{4,5},{5,6},{6,7},{7,8},{8,9},{9,10... | collective-permute-start | bytes 1544 | tf_op jit(solution)/shard_map/while/body/eval_jaxpr/ppermute | solution.py:16
  69.5 8.6 %collective-permute-start = (bf16[128,1024]{1,0:T(8,128)(2,1)S(1)}, bf16[128,1024]{1,0:T(8,128)(2,1)S(1)}, u32[]{:S(2)}, u32[]{:S(2)}) collective-permute-start(bf16[128,1024]{1,0:T(8,128)(2,1)S(1)} %get-tuple-element.260), channel_id=1, source_target_pairs={{15,0},{0,1},{1,2},{2,3},{3,4},{4,5},{5,6},{6,7},{7,8},{8,9},{9,10... | collective-permute-start | bytes 786440 | tf_op jit(solution)/shard_map/while/body/eval_jaxpr/ppermute | solution.py:16
  69.5 8.6 %collective-permute-start.1 = (s32[128]{0:T(128)S(1)}, s32[128]{0:T(128)S(1)}, u32[]{:S(2)}, u32[]{:S(2)}) collective-permute-start(s32[128]{0:T(128)S(1)} %get-tuple-element.261), channel_id=1, source_target_pairs={{15,0},{0,1},{1,2},{2,3},{3,4},{4,5},{5,6},{6,7},{7,8},{8,9},{9,10... | collective-permute-start | bytes 1544 | tf_op jit(solution)/shard_map/while/body/eval_jaxpr/ppermute | solution.py:16
  80.6 8.6 %collective-permute-start = (bf16[128,1024]{1,0:T(8,128)(2,1)S(1)}, bf16[128,1024]{1,0:T(8,128)(2,1)S(1)}, u32[]{:S(2)}, u32[]{:S(2)}) collective-permute-start(bf16[128,1024]{1,0:T(8,128)(2,1)S(1)} %get-tuple-element.260), channel_id=1, source_target_pairs={{15,0},{0,1},{1,2},{2,3},{3,4},{4,5},{5,6},{6,7},{7,8},{8,9},{9,10... | collective-permute-start | bytes 786440 | tf_op jit(solution)/shard_map/while/body/eval_jaxpr/ppermute | solution.py:16
  80.7 8.6 %collective-permute-start.1 = (s32[128]{0:T(128)S(1)}, s32[128]{0:T(128)S(1)}, u32[]{:S(2)}, u32[]{:S(2)}) collective-permute-start(s32[128]{0:T(128)S(1)} %get-tuple-element.261), channel_id=1, source_target_pairs={{15,0},{0,1},{1,2},{2,3},{3,4},{4,5},{5,6},{6,7},{7,8},{8,9},{9,10... | collective-permute-start | bytes 1544 | tf_op jit(solution)/shard_map/while/body/eval_jaxpr/ppermute | solution.py:16
  91.8 8.6 %collective-permute-start = (bf16[128,1024]{1,0:T(8,128)(2,1)S(1)}, bf16[128,1024]{1,0:T(8,128)(2,1)S(1)}, u32[]{:S(2)}, u32[]{:S(2)}) collective-permute-start(bf16[128,1024]{1,0:T(8,128)(2,1)S(1)} %get-tuple-element.260), channel_id=1, source_target_pairs={{15,0},{0,1},{1,2},{2,3},{3,4},{4,5},{5,6},{6,7},{7,8},{8,9},{9,10... | collective-permute-start | bytes 786440 | tf_op jit(solution)/shard_map/while/body/eval_jaxpr/ppermute | solution.py:16
  91.8 8.6 %collective-permute-start.1 = (s32[128]{0:T(128)S(1)}, s32[128]{0:T(128)S(1)}, u32[]{:S(2)}, u32[]{:S(2)}) collective-permute-start(s32[128]{0:T(128)S(1)} %get-tuple-element.261), channel_id=1, source_target_pairs={{15,0},{0,1},{1,2},{2,3},{3,4},{4,5},{5,6},{6,7},{7,8},{8,9},{9,10... | collective-permute-start | bytes 1544 | tf_op jit(solution)/shard_map/while/body/eval_jaxpr/ppermute | solution.py:16
  103.0 8.6 %collective-permute-start = (bf16[128,1024]{1,0:T(8,128)(2,1)S(1)}, bf16[128,1024]{1,0:T(8,128)(2,1)S(1)}, u32[]{:S(2)}, u32[]{:S(2)}) collective-permute-start(bf16[128,1024]{1,0:T(8,128)(2,1)S(1)} %get-tuple-element.260), channel_id=1, source_target_pairs={{15,0},{0,1},{1,2},{2,3},{3,4},{4,5},{5,6},{6,7},{7,8},{8,9},{9,10... | collective-permute-start | bytes 786440 | tf_op jit(solution)/shard_map/while/body/eval_jaxpr/ppermute | solution.py:16
  103.0 8.6 %collective-permute-start.1 = (s32[128]{0:T(128)S(1)}, s32[128]{0:T(128)S(1)}, u32[]{:S(2)}, u32[]{:S(2)}) collective-permute-start(s32[128]{0:T(128)S(1)} %get-tuple-element.261), channel_id=1, source_target_pairs={{15,0},{0,1},{1,2},{2,3},{3,4},{4,5},{5,6},{6,7},{7,8},{8,9},{9,10... | collective-permute-start | bytes 1544 | tf_op jit(solution)/shard_map/while/body/eval_jaxpr/ppermute | solution.py:16
  114.2 8.6 %collective-permute-start = (bf16[128,1024]{1,0:T(8,128)(2,1)S(1)}, bf16[128,1024]{1,0:T(8,128)(2,1)S(1)}, u32[]{:S(2)}, u32[]{:S(2)}) collective-permute-start(bf16[128,1024]{1,0:T(8,128)(2,1)S(1)} %get-tuple-element.260), channel_id=1, source_target_pairs={{15,0},{0,1},{1,2},{2,3},{3,4},{4,5},{5,6},{6,7},{7,8},{8,9},{9,10... | collective-permute-start | bytes 786440 | tf_op jit(solution)/shard_map/while/body/eval_jaxpr/ppermute | solution.py:16
  125.3 8.6 %collective-permute-start = (bf16[128,1024]{1,0:T(8,128)(2,1)S(1)}, bf16[128,1024]{1,0:T(8,128)(2,1)S(1)}, u32[]{:S(2)}, u32[]{:S(2)}) collective-permute-start(bf16[128,1024]{1,0:T(8,128)(2,1)S(1)} %get-tuple-element.260), channel_id=1, source_target_pairs={{15,0},{0,1},{1,2},{2,3},{3,4},{4,5},{5,6},{6,7},{7,8},{8,9},{9,10... | collective-permute-start | bytes 786440 | tf_op jit(solution)/shard_map/while/body/eval_jaxpr/ppermute | solution.py:16
  125.4 8.6 %collective-permute-start.1 = (s32[128]{0:T(128)S(1)}, s32[128]{0:T(128)S(1)}, u32[]{:S(2)}, u32[]{:S(2)}) collective-permute-start(s32[128]{0:T(128)S(1)} %get-tuple-element.261), channel_id=1, source_target_pairs={{15,0},{0,1},{1,2},{2,3},{3,4},{4,5},{5,6},{6,7},{7,8},{8,9},{9,10... | collective-permute-start | bytes 1544 | tf_op jit(solution)/shard_map/while/body/eval_jaxpr/ppermute | solution.py:16
  136.5 8.6 %collective-permute-start = (bf16[128,1024]{1,0:T(8,128)(2,1)S(1)}, bf16[128,1024]{1,0:T(8,128)(2,1)S(1)}, u32[]{:S(2)}, u32[]{:S(2)}) collective-permute-start(bf16[128,1024]{1,0:T(8,128)(2,1)S(1)} %get-tuple-element.260), channel_id=1, source_target_pairs={{15,0},{0,1},{1,2},{2,3},{3,4},{4,5},{5,6},{6,7},{7,8},{8,9},{9,10... | collective-permute-start | bytes 786440 | tf_op jit(solution)/shard_map/while/body/eval_jaxpr/ppermute | solution.py:16
  136.5 8.6 %collective-permute-start.1 = (s32[128]{0:T(128)S(1)}, s32[128]{0:T(128)S(1)}, u32[]{:S(2)}, u32[]{:S(2)}) collective-permute-start(s32[128]{0:T(128)S(1)} %get-tuple-element.261), channel_id=1, source_target_pairs={{15,0},{0,1},{1,2},{2,3},{3,4},{4,5},{5,6},{6,7},{7,8},{8,9},{9,10... | collective-permute-start | bytes 1544 | tf_op jit(solution)/shard_map/while/body/eval_jaxpr/ppermute | solution.py:16
  147.7 8.6 %collective-permute-start = (bf16[128,1024]{1,0:T(8,128)(2,1)S(1)}, bf16[128,1024]{1,0:T(8,128)(2,1)S(1)}, u32[]{:S(2)}, u32[]{:S(2)}) collective-permute-start(bf16[128,1024]{1,0:T(8,128)(2,1)S(1)} %get-tuple-element.260), channel_id=1, source_target_pairs={{15,0},{0,1},{1,2},{2,3},{3,4},{4,5},{5,6},{6,7},{7,8},{8,9},{9,10... | collective-permute-start | bytes 786440 | tf_op jit(solution)/shard_map/while/body/eval_jaxpr/ppermute | solution.py:16
  147.7 8.6 %collective-permute-start.1 = (s32[128]{0:T(128)S(1)}, s32[128]{0:T(128)S(1)}, u32[]{:S(2)}, u32[]{:S(2)}) collective-permute-start(s32[128]{0:T(128)S(1)} %get-tuple-element.261), channel_id=1, source_target_pairs={{15,0},{0,1},{1,2},{2,3},{3,4},{4,5},{5,6},{6,7},{7,8},{8,9},{9,10... | collective-permute-start | bytes 1544 | tf_op jit(solution)/shard_map/while/body/eval_jaxpr/ppermute | solution.py:16
  158.9 8.6 %collective-permute-start = (bf16[128,1024]{1,0:T(8,128)(2,1)S(1)}, bf16[128,1024]{1,0:T(8,128)(2,1)S(1)}, u32[]{:S(2)}, u32[]{:S(2)}) collective-permute-start(bf16[128,1024]{1,0:T(8,128)(2,1)S(1)} %get-tuple-element.260), channel_id=1, source_target_pairs={{15,0},{0,1},{1,2},{2,3},{3,4},{4,5},{5,6},{6,7},{7,8},{8,9},{9,10... | collective-permute-start | bytes 786440 | tf_op jit(solution)/shard_map/while/body/eval_jaxpr/ppermute | solution.py:16
  158.9 8.6 %collective-permute-start.1 = (s32[128]{0:T(128)S(1)}, s32[128]{0:T(128)S(1)}, u32[]{:S(2)}, u32[]{:S(2)}) collective-permute-start(s32[128]{0:T(128)S(1)} %get-tuple-element.261), channel_id=1, source_target_pairs={{15,0},{0,1},{1,2},{2,3},{3,4},{4,5},{5,6},{6,7},{7,8},{8,9},{9,10... | collective-permute-start | bytes 1544 | tf_op jit(solution)/shard_map/while/body/eval_jaxpr/ppermute | solution.py:16
  170.0 8.6 %collective-permute-start = (bf16[128,1024]{1,0:T(8,128)(2,1)S(1)}, bf16[128,1024]{1,0:T(8,128)(2,1)S(1)}, u32[]{:S(2)}, u32[]{:S(2)}) collective-permute-start(bf16[128,1024]{1,0:T(8,128)(2,1)S(1)} %get-tuple-element.260), channel_id=1, source_target_pairs={{15,0},{0,1},{1,2},{2,3},{3,4},{4,5},{5,6},{6,7},{7,8},{8,9},{9,10... | collective-permute-start | bytes 786440 | tf_op jit(solution)/shard_map/while/body/eval_jaxpr/ppermute | solution.py:16
  181.2 8.6 %collective-permute-start = (bf16[128,1024]{1,0:T(8,128)(2,1)S(1)}, bf16[128,1024]{1,0:T(8,128)(2,1)S(1)}, u32[]{:S(2)}, u32[]{:S(2)}) collective-permute-start(bf16[128,1024]{1,0:T(8,128)(2,1)S(1)} %get-tuple-element.260), channel_id=1, source_target_pairs={{15,0},{0,1},{1,2},{2,3},{3,4},{4,5},{5,6},{6,7},{7,8},{8,9},{9,10... | collective-permute-start | bytes 786440 | tf_op jit(solution)/shard_map/while/body/eval_jaxpr/ppermute | solution.py:16
  208.3 18.2 %all-to-all-start.2 = ((f32[16,8,1024]{2,1,0:T(8,128)}), f32[16,8,1024]{2,1,0:T(8,128)S(1)}, u32[]{:S(2)}, u32[]{:S(2)}) async-start(f32[16,8,1024]{2,1,0:T(8,128)} %bitcast.5), calls=%async_computation.2 | async-start | bytes 1048576 | tf_op jit(solution)/shard_map/all_to_all | solution.py:86
  (11 other events, 65.4 us)
where the time goes:
time: 230 us; the launch traced here: 228 us
  waiting for transfers between devices  139 us (60%)
  matrix products  37.8 us (16%)
  starting transfers between devices  20.3 us (9%)
  blocking collectives  15.8 us (7%)
  local copies, waits for them, and re-layouts  8.53 us (4%)
  other arithmetic  5.42 us (2%)
    ppermute x30, waiting for transfers between devices, passed_along(): return lax.ppermute(block, axis, route)  117 us
    dot_general x16, matrix products, absorb(): jnp.dot(weight.astype(jnp.bfloat16), visit_rows, preferred_element_type=j...  33.6 us
    all_to_all x1, blocking collectives, local(): lax.all_to_all(totals.reshape(devices, capacity), 'blk', split_axis=0, co...  15.8 us
    all_to_all x1, waiting for transfers between devices, local(): lax.all_to_all(pulled.reshape(devices, capacity, width), 'blk', split_axi...  11.1 us
    all_to_all x1, waiting for transfers between devices, local(): lax.all_to_all(send_rows.reshape(devices, capacity, width), 'blk', split_...  8.04 us
    all_to_all x1, starting transfers between devices, local(): lax.all_to_all(send_ids.reshape(devices, capacity), 'blk', split_axis=0,...  7.32 us
    ppermute x30, starting transfers between devices, passed_along(): return lax.ppermute(block, axis, route)  4.87 us
  transfers between devices with their start and end apart: 33, of which 18 were waited for; matrix products, arithmetic and copies ran while one was open for 3% of the time, Pallas kernels for 0%

commit v1 on v0

--- a/solution.py
+++ b/solution.py
@@ -1,6 +1,8 @@
 import jax
 import jax.numpy as jnp
 from jax import lax
+from jax.experimental import pallas as pl
+from jax.experimental.pallas import tpu as pltpu
 from jax.sharding import PartitionSpec as P
 
 CYCLE = 16
@@ -97,9 +99,237 @@
     return (neighbour_mean, dup_score)
 
 
+PIECES = 2
+GATHER_DEVICES = 16
+MESH = pl.DeviceIdType.MESH
+
+
+def gather_kernel(emb_ref, ids_ref, mean_ref, score_ref, docs, meta, pulled, totals,
+                  send_sem, recv_sem, meta_send, meta_recv):
+    rows, width = emb_ref.shape
+    piece = rows // PIECES
+    me = lax.axis_index("blk")
+    z, x, core = me // 4, (me // 2) % 2, me % 2
+    z_end = GATHER_DEVICES // 4 - 1
+
+    def slot_of(zz, xx, cc):
+        return zz * 4 + xx * 2 + cc
+
+    barrier = pltpu.get_barrier_semaphore()
+    for step in range(1, GATHER_DEVICES):
+        pl.semaphore_signal(
+            barrier, inc=1, device_id={"blk": (me + step) % GATHER_DEVICES}, device_id_type=MESH
+        )
+
+    own = emb_ref[...]
+    for h in range(PIECES):
+        docs[me, h] = own[h * piece:(h + 1) * piece]
+    own_f = own.astype(jnp.float32)
+    own_norm = jnp.sum(own_f * own_f, 1, keepdims=True)
+    line = lax.broadcasted_iota(jnp.int32, (rows, rows), 0)
+    lane = lax.broadcasted_iota(jnp.int32, (rows, rows), 1)
+    diagonal = line == lane
+    ids_row = ids_ref[...].astype(jnp.float32)
+    own_ids = jnp.sum(jnp.where(diagonal, ids_row, 0.0), 1, keepdims=True)
+    norm_row = jnp.sum(jnp.where(diagonal, own_norm, 0.0), 0, keepdims=True)
+    meta_line = lax.broadcasted_iota(jnp.int32, (8, rows), 0)
+    meta[me] = jnp.where(meta_line == 0, norm_row, ids_row)
+    pulled[...] = jnp.zeros_like(pulled)
+    totals[...] = jnp.zeros_like(totals)
+
+    pl.semaphore_wait(barrier, GATHER_DEVICES - 1)
+
+    sent = []
+
+    def copy(way, slot, h, target):
+        return pltpu.make_async_remote_copy(
+            src_ref=docs.at[slot, h],
+            dst_ref=docs.at[slot, h],
+            send_sem=send_sem.at[way, slot, h],
+            recv_sem=recv_sem.at[slot, h],
+            device_id={"blk": target},
+            device_id_type=MESH,
+        )
+
+    def send(pred, way, slot, h):
+        target = {
+            "up": slot_of(jnp.minimum(z + 1, z_end), x, core),
+            "down": slot_of(jnp.maximum(z - 1, 0), x, core),
+            "x": slot_of(z, 1 - x, core),
+            "core": slot_of(z, x, 1 - core),
+        }[way]
+        index = ("up", "down", "x", "core").index(way)
+
+        def start():
+            copy(index, slot, h, target).start()
+
+        def finish():
+            copy(index, slot, h, target).wait_send()
+
+        if pred is None:
+            start()
+            sent.append(finish)
+        else:
+            pl.when(pred)(start)
+            sent.append(lambda: pl.when(pred)(finish))
+
+    def arrive(slot, h):
+        copy(3, slot, h, slot_of(z, x, 1 - core)).wait_recv()
+
+    def pass_column(zz, h, wait):
+        slot = slot_of(zz, x, core)
+        if wait:
+            arrive(slot, h)
+        send((zz >= z) & (z > 0), "down", slot, h)
+        send((zz <= z) & (z < z_end), "up", slot, h)
+        beside = ((z == 1) & (zz == 0)) | ((z == z_end - 1) & (zz == z_end))
+        far = ((z == 0) & (zz == z_end)) | ((z == z_end) & (zz == 0))
+        skip = (beside | far) if h < PIECES // 2 else beside
+        send(jnp.logical_not(skip), "x", slot, h)
+        send(None, "core", slot, h)
+
+    def pass_other(zz, h):
+        slot = slot_of(zz, 1 - x, core)
+        arrive(slot, h)
+        up = (z == 0) & (zz == 0)
+        down = (z == z_end) & (zz == z_end)
+        if h < PIECES // 2:
+            up = up | ((z == z_end - 1) & (zz == 0))
+            down = down | ((z == 1) & (zz == z_end))
+        send(down, "down", slot, h)
+        send(up, "up", slot, h)
+        send(None, "core", slot, h)
+
+    def meta_copy(step):
+        target = (me + step) % GATHER_DEVICES
+        return pltpu.make_async_remote_copy(
+            src_ref=meta.at[me],
+            dst_ref=meta.at[me],
+            send_sem=meta_send.at[step],
+            recv_sem=meta_recv.at[me],
+            device_id={"blk": target},
+            device_id_type=MESH,
+        )
+
+    def meta_arrive(step):
+        source = (me + step) % GATHER_DEVICES
+        pltpu.make_async_remote_copy(
+            src_ref=meta.at[source],
+            dst_ref=meta.at[source],
+            send_sem=meta_send.at[step],
+            recv_sem=meta_recv.at[source],
+            device_id={"blk": source},
+            device_id_type=MESH,
+        ).wait_recv()
+
+    def absorb(zz, xx, own_chip=False):
+        for h in range(PIECES):
+            arrive(slot_of(zz, xx, 1 - core), h)
+        first = slot_of(zz, xx, 0)
+        visit = docs[pl.ds(first, 2)].reshape(2 * rows, width)
+        info = meta[pl.ds(first, 2)]
+        visit_norm = jnp.concatenate([info[0, 0:1], info[1, 0:1]], 1)
+        visit_ids = jnp.concatenate([info[0, 1:2], info[1, 1:2]], 1)
+        inner = lax.dot_general(
+            emb_ref[...], visit, (((1,), (1,)), ((), ())), preferred_element_type=jnp.float32
+        )
+        distance = jnp.maximum(own_norm + visit_norm - 2.0 * inner, 0.0)
+        allowed = own_ids == visit_ids
+        if own_chip:
+            home = lax.broadcasted_iota(jnp.int32, (rows, 2 * rows), 0) + core * rows
+            away = lax.broadcasted_iota(jnp.int32, (rows, 2 * rows), 1)
+            allowed = allowed & (home != away)
+        weight = jnp.where(allowed, jnp.exp(distance * (-SHARPNESS / width)), 0.0)
+        totals[...] += jnp.sum(weight, 1, keepdims=True)
+        pulled[...] += jnp.dot(
+            weight.astype(jnp.bfloat16), visit, preferred_element_type=jnp.float32
+        )
+
+    z1 = jnp.where(z % 2 == 0, 1, 2)
+    z3 = jnp.where(z < 2, z_end, 0)
+    z2 = 6 - z - z1 - z3
+    halves = range(PIECES)
+
+    for h in halves:
+        pass_column(z, h, False)
+    for step in range(1, GATHER_DEVICES):
+        meta_copy(step).start()
+    for step in range(1, GATHER_DEVICES):
+        meta_arrive(step)
+    absorb(z, x, True)
+    for h in halves:
+        pass_column(z1, h, True)
+    for h in halves:
+        pass_other(z, h)
+    absorb(z1, x)
+    absorb(z, 1 - x)
+    for h in halves:
+        pass_column(z2, h, True)
+    absorb(z2, x)
+    for h in halves:
+        if h < PIECES // 2:
+            pass_column(z3, h, True)
+    for h in halves:
+        pass_other(z1, h)
+    for h in halves:
+        if h >= PIECES // 2:
+            pass_column(z3, h, True)
+    absorb(z1, 1 - x)
+    absorb(z3, x)
+    for h in halves:
+        pass_other(z2, h)
+    absorb(z2, 1 - x)
+    for h in halves:
+        pass_other(z3, h)
+    absorb(z3, 1 - x)
+
+    scale = 1.0 + totals[...]
+    mean_ref[...] = (pulled[...] / scale).astype(jnp.bfloat16)
+    score_ref[...] = jnp.sum(jnp.where(diagonal, jnp.log(scale), 0.0), 0, keepdims=True)
+    for finish in sent:
+        finish()
+    for step in range(1, GATHER_DEVICES):
+        meta_copy(step).wait_send()
+
+
+def gathered(emb, cluster):
+    rows, width = emb.shape
+    devices = GATHER_DEVICES
+    vmem = pl.BlockSpec(memory_space=pltpu.VMEM)
+    mean, score = pl.pallas_call(
+        gather_kernel,
+        out_shape=(
+            jax.ShapeDtypeStruct((rows, width), jnp.bfloat16),
+            jax.ShapeDtypeStruct((1, rows), jnp.float32),
+        ),
+        in_specs=[vmem, vmem],
+        out_specs=(vmem, vmem),
+        scratch_shapes=[
+            pltpu.VMEM((devices, PIECES, rows // PIECES, width), jnp.bfloat16),
+            pltpu.VMEM((devices, 8, rows), jnp.float32),
+            pltpu.VMEM((rows, width), jnp.float32),
+            pltpu.VMEM((rows, 1), jnp.float32),
+            pltpu.SemaphoreType.DMA((4, devices, PIECES)),
+            pltpu.SemaphoreType.DMA((devices, PIECES)),
+            pltpu.SemaphoreType.DMA((devices,)),
+            pltpu.SemaphoreType.DMA((devices,)),
+        ],
+        compiler_params=pltpu.CompilerParams(
+            collective_id=0, has_side_effects=True, vmem_limit_bytes=40 << 20
+        ),
+        cost_estimate=pl.CostEstimate(
+            flops=4 * devices * rows * rows * width,
+            bytes_accessed=4 * rows * width,
+            transcendentals=devices * rows * rows,
+        ),
+    )(emb, cluster.reshape(1, rows))
+    return mean, score.reshape(rows)
+
+
 def solution(mesh):
+    small = mesh.shape["blk"] == GATHER_DEVICES
     return jax.shard_map(
-        local,
+        gathered if small else local,
         mesh=mesh,
         in_specs=(P(("parts", "blk"), None), P(("parts", "blk"))),
         out_specs=(P(("parts", "blk"), None), P(("parts", "blk"))),

time: 230 us -> 41.5 us (0.18)
  waiting for transfers between devices: 139 us -> 0 us
  Pallas kernels: 0 us -> 37.9 us
  matrix products: 37.8 us -> 0 us
  starting transfers between devices: 20.3 us -> 0 us
  blocking collectives: 15.8 us -> 0 us
  local copies, waits for them, and re-layouts: 8.53 us -> 2.81 us
  other arithmetic: 5.42 us -> 0 us
    ppermute x30 -> x0, waiting for transfers between devices: 117 us -> none  [passed_along(): return lax.ppermute(block, axis, route)]
    pallas_call x0 -> x1, Pallas kernels: none -> 37.9 us  [gathered(): pl.pallas_call(gather_kernel, out_shape=(jax.ShapeDtypeStruct((rows, widt...]
    dot_general x32 -> x0, matrix products: 37.8 us -> none  [the longest x16 33.6 us: absorb(): jnp.dot(weight.astype(jnp.bfloat16), visit_rows, preferred_element_type=j...]
    all_to_all x3 -> x0, waiting for transfers between devices: 22.7 us -> none  [the longest x1 11.1 us: local(): lax.all_to_all(pulled.reshape(devices, capacity, width), 'blk', split_axi...]
    all_to_all x1 -> x0, blocking collectives: 15.8 us -> none  [local(): lax.all_to_all(totals.reshape(devices, capacity), 'blk', split_axis=0, co...]
    all_to_all x3 -> x0, starting transfers between devices: 15.4 us -> none  [the longest x1 7.32 us: local(): lax.all_to_all(send_ids.reshape(devices, capacity), 'blk', split_axis=0,...]
    ppermute x30 -> x0, starting transfers between devices: 4.87 us -> none  [passed_along(): return lax.ppermute(block, axis, route)]
    scatter x2 -> x0, local copies, waits for them, and re-layouts: 3.2 us -> none  [the longest x1 2.22 us: local(): send_rows = jnp.zeros((slots, width), jnp.bfloat16).at[slot_index].set(emb)]
  transfers between devices with their start and end apart: 33 -> 0, of which waited for: 18 -> 0; matrix products, arithmetic and copies ran while one was open for 3% -> 0% of each run, Pallas kernels for 0% -> 0%
where the time goes in v1:
time: 41.5 us; the launch traced here: 41.4 us
  Pallas kernels  37.9 us (91%)
  local copies, waits for them, and re-layouts  2.81 us (7%)
  between operations  0.65 us (2%)
    pallas_call x1, Pallas kernels, gathered(): pl.pallas_call(gather_kernel, out_shape=(jax.ShapeDtypeStruct((rows, widt...  37.9 us
    unnamed x6, local copies, waits for them, and re-layouts  2.81 us

profile of v1, /device:TPU:1, one launch (start us, length us, event | category | flops | bytes accessed | tf_op | source)
XLA Modules:
  0.0 41.4 jit_solution(6900880667341614977)
XLA Ops:
  0.6 0.0 copy-start.1
  0.6 0.6 %copy-done.1 = s32[128]{0:T(128)S(1)} copy-done((s32[128]{0:T(128)S(1)}, s32[128]{0:T(128)}, u32[]{:S(2)}) %copy-start.1) | copy-done | bytes 536
  1.3 0.0 copy-start
  1.3 0.9 %copy-done = bf16[128,1024]{1,0:T(8,128)(2,1)S(1)} copy-done((bf16[128,1024]{1,0:T(8,128)(2,1)S(1)}, bf16[128,1024]{1,0:T(8,128)(2,1)}, u32[]{:S(2)}) %copy-start) | copy-done | bytes 262168
  2.2 37.9 %shard_map.41 = (bf16[128,1024]{1,0:T(8,128)(2,1)S(1)}, f32[1,128]{1,0:T(1,128)S(1)}) custom-call(bf16[128,1024]{1,0:T(8,128)(2,1)S(1)} %copy-done, s32[1,128]{1,0:T(1,128)S(1)} %bitcast.2), custom_call_target="tpu_custom_call" | custom-call | flops 1073741824 | bytes 524288 | tf_op jit(solution)/shard_map/pallas_call | solution.py:299
  40.2 0.7 %copy.6 = bf16[128,1024]{1,0:T(8,128)(2,1)} copy(bf16[128,1024]{1,0:T(8,128)(2,1)S(1)} %get-tuple-element.8) | data formatting | bytes 524288
  40.9 0.5 %copy.7 = f32[128]{0:T(128)} copy(f32[128]{0:T(128)S(1)} %bitcast.3) | data formatting | bytes 1024
Async XLA Ops:
  0.6 0.7 %copy-start.1 = (s32[128]{0:T(128)S(1)}, s32[128]{0:T(128)}, u32[]{:S(2)}) copy-start(s32[128]{0:T(128)} %param.3) | copy-start | bytes 1540
  1.3 0.9 %copy-start = (bf16[128,1024]{1,0:T(8,128)(2,1)S(1)}, bf16[128,1024]{1,0:T(8,128)(2,1)}, u32[]{:S(2)}) copy-start(bf16[128,1024]{1,0:T(8,128)(2,1)} %emb_ref.1) | copy-start | bytes 786436

commit v2 on v1

--- a/solution.py
+++ b/solution.py
@@ -104,8 +104,8 @@
 MESH = pl.DeviceIdType.MESH
 
 
-def gather_kernel(emb_ref, ids_ref, mean_ref, score_ref, docs, meta, pulled, totals,
-                  send_sem, recv_sem, meta_send, meta_recv):
+def gather_kernel(emb_ref, cluster_ref, mean_ref, score_ref, docs, meta, ids_ref, pulled, totals,
+                  load_sem, send_sem, recv_sem, meta_send, meta_recv):
     rows, width = emb_ref.shape
     piece = rows // PIECES
     me = lax.axis_index("blk")
@@ -115,15 +115,41 @@
     def slot_of(zz, xx, cc):
         return zz * 4 + xx * 2 + cc
 
+    ways = ("up", "down", "x", "core")
+    neighbour = {
+        "up": slot_of(jnp.minimum(z + 1, z_end), x, core),
+        "down": slot_of(jnp.maximum(z - 1, 0), x, core),
+        "x": slot_of(z, 1 - x, core),
+        "core": slot_of(z, x, 1 - core),
+    }
+
     barrier = pltpu.get_barrier_semaphore()
-    for step in range(1, GATHER_DEVICES):
+
+    def greet(way):
         pl.semaphore_signal(
-            barrier, inc=1, device_id={"blk": (me + step) % GATHER_DEVICES}, device_id_type=MESH
-        )
-
-    own = emb_ref[...]
+            barrier, inc=1, device_id={"blk": neighbour[way]}, device_id_type=MESH
+        )
+
+    pl.when(z > 0)(lambda: greet("down"))
+    pl.when(z < z_end)(lambda: greet("up"))
+    greet("x")
+    greet("core")
+
+    loads = [pltpu.make_async_copy(cluster_ref, ids_ref, load_sem.at[PIECES])]
     for h in range(PIECES):
-        docs[me, h] = own[h * piece:(h + 1) * piece]
+        loads.append(
+            pltpu.make_async_copy(
+                emb_ref.at[pl.ds(h * piece, piece)], docs.at[me, h], load_sem.at[h]
+            )
+        )
+    for load in loads:
+        load.start()
+    pulled[...] = jnp.zeros_like(pulled)
+    totals[...] = jnp.zeros_like(totals)
+    for load in loads:
+        load.wait()
+
+    own = docs[me].reshape(rows, width)
     own_f = own.astype(jnp.float32)
     own_norm = jnp.sum(own_f * own_f, 1, keepdims=True)
     line = lax.broadcasted_iota(jnp.int32, (rows, rows), 0)
@@ -134,10 +160,8 @@
     norm_row = jnp.sum(jnp.where(diagonal, own_norm, 0.0), 0, keepdims=True)
     meta_line = lax.broadcasted_iota(jnp.int32, (8, rows), 0)
     meta[me] = jnp.where(meta_line == 0, norm_row, ids_row)
-    pulled[...] = jnp.zeros_like(pulled)
-    totals[...] = jnp.zeros_like(totals)
-
-    pl.semaphore_wait(barrier, GATHER_DEVICES - 1)
+
+    pl.semaphore_wait(barrier, jnp.where((z > 0) & (z < z_end), 4, 3))
 
     sent = []
 
@@ -151,76 +175,68 @@
             device_id_type=MESH,
         )
 
+    def meta_copy(way, slot, target):
+        return pltpu.make_async_remote_copy(
+            src_ref=meta.at[slot],
+            dst_ref=meta.at[slot],
+            send_sem=meta_send.at[way, slot],
+            recv_sem=meta_recv.at[slot],
+            device_id={"blk": target},
+            device_id_type=MESH,
+        )
+
     def send(pred, way, slot, h):
-        target = {
-            "up": slot_of(jnp.minimum(z + 1, z_end), x, core),
-            "down": slot_of(jnp.maximum(z - 1, 0), x, core),
-            "x": slot_of(z, 1 - x, core),
-            "core": slot_of(z, x, 1 - core),
-        }[way]
-        index = ("up", "down", "x", "core").index(way)
+        index = ways.index(way)
+        target = neighbour[way]
 
         def start():
+            if h == PIECES - 1:
+                meta_copy(index, slot, target).start()
             copy(index, slot, h, target).start()
 
         def finish():
+            if h == PIECES - 1:
+                meta_copy(index, slot, target).wait_send()
             copy(index, slot, h, target).wait_send()
 
-        if pred is None:
-            start()
-            sent.append(finish)
-        else:
-            pl.when(pred)(start)
-            sent.append(lambda: pl.when(pred)(finish))
+        pl.when(pred)(start)
+        sent.append(lambda: pl.when(pred)(finish))
 
     def arrive(slot, h):
-        copy(3, slot, h, slot_of(z, x, 1 - core)).wait_recv()
-
-    def pass_column(zz, h, wait):
+        if h == PIECES - 1:
+            meta_copy(3, slot, neighbour["core"]).wait_recv()
+        copy(3, slot, h, neighbour["core"]).wait_recv()
+
+    def to_line(zz, h):
         slot = slot_of(zz, x, core)
-        if wait:
-            arrive(slot, h)
         send((zz >= z) & (z > 0), "down", slot, h)
         send((zz <= z) & (z < z_end), "up", slot, h)
-        beside = ((z == 1) & (zz == 0)) | ((z == z_end - 1) & (zz == z_end))
-        far = ((z == 0) & (zz == z_end)) | ((z == z_end) & (zz == 0))
-        skip = (beside | far) if h < PIECES // 2 else beside
-        send(jnp.logical_not(skip), "x", slot, h)
-        send(None, "core", slot, h)
-
-    def pass_other(zz, h):
+
+    def to_side(zz, h):
+        from_low, from_high = (zz == 0) & (z > 0), (zz == z_end) & (z < z_end)
+        if h >= PIECES // 2:
+            from_low = from_low & (z == 1)
+            from_high = from_high & (z == z_end - 1)
+        send(jnp.logical_not(from_low | from_high), "x", slot_of(zz, x, core), h)
+
+    def to_core(zz, xx, h, only):
+        send(only, "core", slot_of(zz, xx, core), h)
+
+    def pass_column(zz, h):
+        arrive(slot_of(zz, x, core), h)
+        to_line(zz, h)
+        to_side(zz, h)
+        to_core(zz, x, h, always)
+
+    def pass_other(zz, h, only):
         slot = slot_of(zz, 1 - x, core)
-        arrive(slot, h)
-        up = (z == 0) & (zz == 0)
-        down = (z == z_end) & (zz == z_end)
-        if h < PIECES // 2:
-            up = up | ((z == z_end - 1) & (zz == 0))
-            down = down | ((z == 1) & (zz == z_end))
-        send(down, "down", slot, h)
-        send(up, "up", slot, h)
-        send(None, "core", slot, h)
-
-    def meta_copy(step):
-        target = (me + step) % GATHER_DEVICES
-        return pltpu.make_async_remote_copy(
-            src_ref=meta.at[me],
-            dst_ref=meta.at[me],
-            send_sem=meta_send.at[step],
-            recv_sem=meta_recv.at[me],
-            device_id={"blk": target},
-            device_id_type=MESH,
-        )
-
-    def meta_arrive(step):
-        source = (me + step) % GATHER_DEVICES
-        pltpu.make_async_remote_copy(
-            src_ref=meta.at[source],
-            dst_ref=meta.at[source],
-            send_sem=meta_send.at[step],
-            recv_sem=meta_recv.at[source],
-            device_id={"blk": source},
-            device_id_type=MESH,
-        ).wait_recv()
+        pl.when(only)(lambda: arrive(slot, h))
+        up, down = (zz == 0) & only, (zz == z_end) & only
+        if h >= PIECES // 2:
+            up, down = up & (z == 0), down & (z == z_end)
+        send(down & (z > 0), "down", slot, h)
+        send(up & (z < z_end), "up", slot, h)
+        to_core(zz, 1 - x, h, only)
 
     def absorb(zz, xx, own_chip=False):
         for h in range(PIECES):
@@ -231,7 +247,10 @@
         visit_norm = jnp.concatenate([info[0, 0:1], info[1, 0:1]], 1)
         visit_ids = jnp.concatenate([info[0, 1:2], info[1, 1:2]], 1)
         inner = lax.dot_general(
-            emb_ref[...], visit, (((1,), (1,)), ((), ())), preferred_element_type=jnp.float32
+            docs[me].reshape(rows, width),
+            visit,
+            (((1,), (1,)), ((), ())),
+            preferred_element_type=jnp.float32,
         )
         distance = jnp.maximum(own_norm + visit_norm - 2.0 * inner, 0.0)
         allowed = own_ids == visit_ids
@@ -248,39 +267,49 @@
     z1 = jnp.where(z % 2 == 0, 1, 2)
     z3 = jnp.where(z < 2, z_end, 0)
     z2 = 6 - z - z1 - z3
-    halves = range(PIECES)
-
-    for h in halves:
-        pass_column(z, h, False)
-    for step in range(1, GATHER_DEVICES):
-        meta_copy(step).start()
-    for step in range(1, GATHER_DEVICES):
-        meta_arrive(step)
+    early = range(PIECES // 2)
+    late = range(PIECES // 2, PIECES)
+    middle = (z > 0) & (z < z_end)
+    end = jnp.logical_not(middle)
+    always = z >= 0
+
+    for h in (*late, *early):
+        to_line(z, h)
+    for h in (*early, *late):
+        to_side(z, h)
+    for h in (*late, *early):
+        to_core(z, x, h, always)
     absorb(z, x, True)
-    for h in halves:
-        pass_column(z1, h, True)
-    for h in halves:
-        pass_other(z, h)
+    for h in (*late, *early):
+        pass_column(z1, h)
+    for h in (*early, *late):
+        pass_other(z, h, always)
     absorb(z1, x)
     absorb(z, 1 - x)
-    for h in halves:
-        pass_column(z2, h, True)
+    for h in (*late, *early):
+        pass_column(z2, h)
     absorb(z2, x)
-    for h in halves:
-        if h < PIECES // 2:
-            pass_column(z3, h, True)
-    for h in halves:
-        pass_other(z1, h)
-    for h in halves:
-        if h >= PIECES // 2:
-            pass_column(z3, h, True)
+    for h in early:
+        pass_other(z2, h, middle)
+    for h in late:
+        pass_column(z3, h)
+    for h in (*late, *early):
+        pass_other(z1, h, always)
+    for h in early:
+        pass_column(z3, h)
     absorb(z1, 1 - x)
+    for h in late:
+        pass_other(z2, h, always)
+    for h in early:
+        pass_other(z2, h, end)
+    for h in early:
+        pass_other(z3, h, middle)
     absorb(z3, x)
-    for h in halves:
-        pass_other(z2, h)
     absorb(z2, 1 - x)
-    for h in halves:
-        pass_other(z3, h)
+    for h in late:
+        pass_other(z3, h, always)
+    for h in early:
+        pass_other(z3, h, end)
     absorb(z3, 1 - x)
 
     scale = 1.0 + totals[...]
@@ -288,8 +317,6 @@
     score_ref[...] = jnp.sum(jnp.where(diagonal, jnp.log(scale), 0.0), 0, keepdims=True)
     for finish in sent:
         finish()
-    for step in range(1, GATHER_DEVICES):
-        meta_copy(step).wait_send()
 
 
 def gathered(emb, cluster):
@@ -302,16 +329,18 @@
             jax.ShapeDtypeStruct((rows, width), jnp.bfloat16),
             jax.ShapeDtypeStruct((1, rows), jnp.float32),
         ),
-        in_specs=[vmem, vmem],
+        in_specs=[pl.BlockSpec(memory_space=pl.ANY)] * 2,
         out_specs=(vmem, vmem),
         scratch_shapes=[
             pltpu.VMEM((devices, PIECES, rows // PIECES, width), jnp.bfloat16),
             pltpu.VMEM((devices, 8, rows), jnp.float32),
+            pltpu.VMEM((1, rows), jnp.int32),
             pltpu.VMEM((rows, width), jnp.float32),
             pltpu.VMEM((rows, 1), jnp.float32),
+            pltpu.SemaphoreType.DMA((PIECES + 1,)),
             pltpu.SemaphoreType.DMA((4, devices, PIECES)),
             pltpu.SemaphoreType.DMA((devices, PIECES)),
-            pltpu.SemaphoreType.DMA((devices,)),
+            pltpu.SemaphoreType.DMA((4, devices)),
             pltpu.SemaphoreType.DMA((devices,)),
         ],
         compiler_params=pltpu.CompilerParams(

time: 41.5 us -> 37.9 us (0.913)
  Pallas kernels: 37.9 us -> 34 us
    pallas_call x1, Pallas kernels: 37.9 us -> 34 us  [gathered(): pl.pallas_call(gather_kernel, out_shape=(jax.ShapeDtypeStruct((rows, widt...]
where the time goes in v2:
time: 37.9 us; the launch traced here: 37.5 us
  Pallas kernels  34 us (90%)
  local copies, waits for them, and re-layouts  2.81 us (7%)
  between operations  0.65 us (2%)
    pallas_call x1, Pallas kernels, gathered(): pl.pallas_call(gather_kernel, out_shape=(jax.ShapeDtypeStruct((rows, widt...  34 us
    unnamed x6, local copies, waits for them, and re-layouts  2.81 us

profile of v2, /device:TPU:1, one launch (start us, length us, event | category | flops | bytes accessed | tf_op | source)
XLA Modules:
  0.0 37.5 jit_solution(6889201063248813164)
XLA Ops:
  0.6 0.0 copy-start.1
  0.6 0.6 %copy-done.1 = s32[128]{0:T(128)S(1)} copy-done((s32[128]{0:T(128)S(1)}, s32[128]{0:T(128)}, u32[]{:S(2)}) %copy-start.1) | copy-done | bytes 536
  1.3 0.0 copy-start
  1.3 0.9 %copy-done = bf16[128,1024]{1,0:T(8,128)(2,1)S(1)} copy-done((bf16[128,1024]{1,0:T(8,128)(2,1)S(1)}, bf16[128,1024]{1,0:T(8,128)(2,1)}, u32[]{:S(2)}) %copy-start) | copy-done | bytes 262168
  2.2 34.0 %shard_map.41 = (bf16[128,1024]{1,0:T(8,128)(2,1)S(1)}, f32[1,128]{1,0:T(1,128)S(1)}) custom-call(bf16[128,1024]{1,0:T(8,128)(2,1)S(1)} %copy-done, s32[1,128]{1,0:T(1,128)S(1)} %bitcast.2), custom_call_target="tpu_custom_call" | custom-call | flops 1073741824 | bytes 524288 | tf_op jit(solution)/shard_map/pallas_call | solution.py:326
  36.3 0.7 %copy.6 = bf16[128,1024]{1,0:T(8,128)(2,1)} copy(bf16[128,1024]{1,0:T(8,128)(2,1)S(1)} %get-tuple-element.8) | data formatting | bytes 524288
  37.0 0.5 %copy.7 = f32[128]{0:T(128)} copy(f32[128]{0:T(128)S(1)} %bitcast.3) | data formatting | bytes 1024
Async XLA Ops:
  0.6 0.7 %copy-start.1 = (s32[128]{0:T(128)S(1)}, s32[128]{0:T(128)}, u32[]{:S(2)}) copy-start(s32[128]{0:T(128)} %param.3) | copy-start | bytes 1540
  1.3 0.9 %copy-start = (bf16[128,1024]{1,0:T(8,128)(2,1)S(1)}, bf16[128,1024]{1,0:T(8,128)(2,1)}, u32[]{:S(2)}) copy-start(bf16[128,1024]{1,0:T(8,128)(2,1)} %emb_ref.1) | copy-start | bytes 786436

commit v3 on v2

--- a/solution.py
+++ b/solution.py
@@ -219,24 +219,24 @@
             from_high = from_high & (z == z_end - 1)
         send(jnp.logical_not(from_low | from_high), "x", slot_of(zz, x, core), h)
 
-    def to_core(zz, xx, h, only):
-        send(only, "core", slot_of(zz, xx, core), h)
+    def to_core(zz, xx, h):
+        send(z >= 0, "core", slot_of(zz, xx, core), h)
 
     def pass_column(zz, h):
         arrive(slot_of(zz, x, core), h)
         to_line(zz, h)
         to_side(zz, h)
-        to_core(zz, x, h, always)
-
-    def pass_other(zz, h, only):
+        to_core(zz, x, h)
+
+    def pass_other(zz, h):
         slot = slot_of(zz, 1 - x, core)
-        pl.when(only)(lambda: arrive(slot, h))
-        up, down = (zz == 0) & only, (zz == z_end) & only
+        arrive(slot, h)
+        up, down = zz == 0, zz == z_end
         if h >= PIECES // 2:
             up, down = up & (z == 0), down & (z == z_end)
         send(down & (z > 0), "down", slot, h)
         send(up & (z < z_end), "up", slot, h)
-        to_core(zz, 1 - x, h, only)
+        to_core(zz, 1 - x, h)
 
     def absorb(zz, xx, own_chip=False):
         for h in range(PIECES):
@@ -269,54 +269,75 @@
     z2 = 6 - z - z1 - z3
     early = range(PIECES // 2)
     late = range(PIECES // 2, PIECES)
+
+    def column(zz, pieces):
+        for h in pieces:
+            pass_column(zz, h)
+
+    def other(zz, pieces):
+        for h in pieces:
+            pass_other(zz, h)
+
+    def begin():
+        for h in (*late, *early):
+            to_line(z, h)
+        for h in (*early, *late):
+            to_side(z, h)
+        for h in (*late, *early):
+            to_core(z, x, h)
+        absorb(z, x, True)
+
+    def at_end():
+        begin()
+        column(z1, (*late, *early))
+        other(z, (*early, *late))
+        absorb(z1, x)
+        column(z2, (*late, *early))
+        other(z1, (*late, *early))
+        absorb(z, 1 - x)
+        absorb(z2, x)
+        column(z3, late)
+        absorb(z1, 1 - x)
+        other(z2, (*late, *early))
+        column(z3, early)
+        absorb(z2, 1 - x)
+        absorb(z3, x)
+        other(z3, (*late, *early))
+        absorb(z3, 1 - x)
+        close()
+
+    def at_middle():
+        begin()
+        column(z1, (*late, *early))
+        column(z2, (*late, *early))
+        other(z, (*early, *late))
+        absorb(z1, x)
+        other(z2, early)
+        column(z3, late)
+        absorb(z2, x)
+        column(z3, early)
+        other(z1, (*late, *early))
+        other(z2, late)
+        absorb(z, 1 - x)
+        other(z3, early)
+        absorb(z1, 1 - x)
+        absorb(z3, x)
+        absorb(z2, 1 - x)
+        other(z3, late)
+        absorb(z3, 1 - x)
+        close()
+
+    def close():
+        scale = 1.0 + totals[...]
+        mean_ref[...] = (pulled[...] / scale).astype(jnp.bfloat16)
+        score_ref[...] = jnp.sum(jnp.where(diagonal, jnp.log(scale), 0.0), 0, keepdims=True)
+        for finish in sent:
+            finish()
+        sent.clear()
+
     middle = (z > 0) & (z < z_end)
-    end = jnp.logical_not(middle)
-    always = z >= 0
-
-    for h in (*late, *early):
-        to_line(z, h)
-    for h in (*early, *late):
-        to_side(z, h)
-    for h in (*late, *early):
-        to_core(z, x, h, always)
-    absorb(z, x, True)
-    for h in (*late, *early):
-        pass_column(z1, h)
-    for h in (*early, *late):
-        pass_other(z, h, always)
-    absorb(z1, x)
-    absorb(z, 1 - x)
-    for h in (*late, *early):
-        pass_column(z2, h)
-    absorb(z2, x)
-    for h in early:
-        pass_other(z2, h, middle)
-    for h in late:
-        pass_column(z3, h)
-    for h in (*late, *early):
-        pass_other(z1, h, always)
-    for h in early:
-        pass_column(z3, h)
-    absorb(z1, 1 - x)
-    for h in late:
-        pass_other(z2, h, always)
-    for h in early:
-        pass_other(z2, h, end)
-    for h in early:
-        pass_other(z3, h, middle)
-    absorb(z3, x)
-    absorb(z2, 1 - x)
-    for h in late:
-        pass_other(z3, h, always)
-    for h in early:
-        pass_other(z3, h, end)
-    absorb(z3, 1 - x)
-
-    scale = 1.0 + totals[...]
-    mean_ref[...] = (pulled[...] / scale).astype(jnp.bfloat16)
-    score_ref[...] = jnp.sum(jnp.where(diagonal, jnp.log(scale), 0.0), 0, keepdims=True)
-    for finish in sent:
-        finish()
+    pl.when(middle)(at_middle)
+    pl.when(jnp.logical_not(middle))(at_end)
 
 
 def gathered(emb, cluster):

time: 37.9 us -> 33.3 us (0.88)
  Pallas kernels: 34 us -> 29.6 us
    pallas_call x1, Pallas kernels: 34 us -> 29.6 us  [gathered(): pl.pallas_call(gather_kernel, out_shape=(jax.ShapeDtypeStruct((rows, widt...]
where the time goes in v3:
time: 33.3 us; the launch traced here: 33.1 us
  Pallas kernels  29.6 us (89%)
  local copies, waits for them, and re-layouts  2.81 us (8%)
  between operations  0.65 us (2%)
    pallas_call x1, Pallas kernels, gathered(): pl.pallas_call(gather_kernel, out_shape=(jax.ShapeDtypeStruct((rows, widt...  29.6 us
    unnamed x6, local copies, waits for them, and re-layouts  2.81 us

profile of v3, /device:TPU:1, one launch (start us, length us, event | category | flops | bytes accessed | tf_op | source)
XLA Modules:
  0.0 33.1 jit_solution(7967067851753979260)
XLA Ops:
  0.6 0.0 copy-start.1
  0.6 0.6 %copy-done.1 = s32[128]{0:T(128)S(1)} copy-done((s32[128]{0:T(128)S(1)}, s32[128]{0:T(128)}, u32[]{:S(2)}) %copy-start.1) | copy-done | bytes 536
  1.3 0.0 copy-start
  1.3 0.9 %copy-done = bf16[128,1024]{1,0:T(8,128)(2,1)S(1)} copy-done((bf16[128,1024]{1,0:T(8,128)(2,1)S(1)}, bf16[128,1024]{1,0:T(8,128)(2,1)}, u32[]{:S(2)}) %copy-start) | copy-done | bytes 262168
  2.2 29.6 %shard_map.41 = (bf16[128,1024]{1,0:T(8,128)(2,1)S(1)}, f32[1,128]{1,0:T(1,128)S(1)}) custom-call(bf16[128,1024]{1,0:T(8,128)(2,1)S(1)} %copy-done, s32[1,128]{1,0:T(1,128)S(1)} %bitcast.2), custom_call_target="tpu_custom_call" | custom-call | flops 1073741824 | bytes 524288 | tf_op jit(solution)/shard_map/pallas_call | solution.py:347
  31.9 0.7 %copy.6 = bf16[128,1024]{1,0:T(8,128)(2,1)} copy(bf16[128,1024]{1,0:T(8,128)(2,1)S(1)} %get-tuple-element.8) | data formatting | bytes 524288
  32.6 0.5 %copy.7 = f32[128]{0:T(128)} copy(f32[128]{0:T(128)S(1)} %bitcast.3) | data formatting | bytes 1024
Async XLA Ops:
  0.6 0.7 %copy-start.1 = (s32[128]{0:T(128)S(1)}, s32[128]{0:T(128)}, u32[]{:S(2)}) copy-start(s32[128]{0:T(128)} %param.3) | copy-start | bytes 1540
  1.3 0.9 %copy-start = (bf16[128,1024]{1,0:T(8,128)(2,1)S(1)}, bf16[128,1024]{1,0:T(8,128)(2,1)}, u32[]{:S(2)}) copy-start(bf16[128,1024]{1,0:T(8,128)(2,1)} %emb_ref.1) | copy-start | bytes 786436

commit v4 on v3

--- a/solution.py
+++ b/solution.py
@@ -365,7 +365,7 @@
             pltpu.SemaphoreType.DMA((devices,)),
         ],
         compiler_params=pltpu.CompilerParams(
-            collective_id=0, has_side_effects=True, vmem_limit_bytes=40 << 20
+            collective_id=0, has_side_effects=True, vmem_limit_bytes=107 << 19
         ),
         cost_estimate=pl.CostEstimate(
             flops=4 * devices * rows * rows * width,

time: 33.3 us -> 32.3 us (0.970)
  local copies, waits for them, and re-layouts: 2.81 us -> 1.86 us
    unnamed x6 -> x4, local copies, waits for them, and re-layouts: 2.81 us -> 1.86 us
where the time goes in v4:
time: 32.3 us; the launch traced here: 32.1 us
  Pallas kernels  29.6 us (92%)
  local copies, waits for them, and re-layouts  1.86 us (6%)
  between operations  0.65 us (2%)
    pallas_call x1, Pallas kernels, gathered(): pl.pallas_call(gather_kernel, out_shape=(jax.ShapeDtypeStruct((rows, widt...  29.6 us
    unnamed x4, local copies, waits for them, and re-layouts  1.86 us

profile of v4, /device:TPU:1, one launch (start us, length us, event | category | flops | bytes accessed | tf_op | source)
XLA Modules:
  0.0 32.1 jit_solution(4665430970044553392)
XLA Ops:
  0.6 0.0 copy-start
  0.6 0.6 %copy-done = s32[128]{0:T(128)S(1)} copy-done((s32[128]{0:T(128)S(1)}, s32[128]{0:T(128)}, u32[]{:S(2)}) %copy-start) | copy-done | bytes 536
  1.3 29.6 %shard_map.41 = (bf16[128,1024]{1,0:T(8,128)(2,1)S(1)}, f32[1,128]{1,0:T(1,128)S(1)}) custom-call(bf16[128,1024]{1,0:T(8,128)(2,1)} %emb_ref.1, s32[1,128]{1,0:T(1,128)S(1)} %bitcast.2), custom_call_target="tpu_custom_call" | custom-call | flops 1073741824 | bytes 524288 | tf_op jit(solution)/shard_map/pallas_call | solution.py:347
  30.9 0.7 %copy.6 = bf16[128,1024]{1,0:T(8,128)(2,1)} copy(bf16[128,1024]{1,0:T(8,128)(2,1)S(1)} %get-tuple-element.8) | data formatting | bytes 524288
  31.6 0.5 %copy.7 = f32[128]{0:T(128)} copy(f32[128]{0:T(128)S(1)} %bitcast.3) | data formatting | bytes 1024
Async XLA Ops:
  0.6 0.7 %copy-start = (s32[128]{0:T(128)S(1)}, s32[128]{0:T(128)}, u32[]{:S(2)}) copy-start(s32[128]{0:T(128)} %param.3) | copy-start | bytes 1540

commit v5 on v4

--- a/solution.py
+++ b/solution.py
@@ -169,7 +169,7 @@
         return pltpu.make_async_remote_copy(
             src_ref=docs.at[slot, h],
             dst_ref=docs.at[slot, h],
-            send_sem=send_sem.at[way, slot, h],
+            send_sem=send_sem.at[way, slot // 2, h],
             recv_sem=recv_sem.at[slot, h],
             device_id={"blk": target},
             device_id_type=MESH,
@@ -179,7 +179,7 @@
         return pltpu.make_async_remote_copy(
             src_ref=meta.at[slot],
             dst_ref=meta.at[slot],
-            send_sem=meta_send.at[way, slot],
+            send_sem=meta_send.at[way, slot // 2],
             recv_sem=meta_recv.at[slot],
             device_id={"blk": target},
             device_id_type=MESH,
@@ -359,9 +359,9 @@
             pltpu.VMEM((rows, width), jnp.float32),
             pltpu.VMEM((rows, 1), jnp.float32),
             pltpu.SemaphoreType.DMA((PIECES + 1,)),
-            pltpu.SemaphoreType.DMA((4, devices, PIECES)),
+            pltpu.SemaphoreType.DMA((4, devices // 2, PIECES)),
             pltpu.SemaphoreType.DMA((devices, PIECES)),
-            pltpu.SemaphoreType.DMA((4, devices)),
+            pltpu.SemaphoreType.DMA((4, devices // 2)),
             pltpu.SemaphoreType.DMA((devices,)),
         ],
         compiler_params=pltpu.CompilerParams(

time: 32.3 us -> 31.4 us (0.972)
  Pallas kernels: 29.6 us -> 28.8 us
    pallas_call x1, Pallas kernels: 29.6 us -> 28.8 us  [gathered(): pl.pallas_call(gather_kernel, out_shape=(jax.ShapeDtypeStruct((rows, widt...]
where the time goes in v5:
time: 31.4 us; the launch traced here: 31.3 us
  Pallas kernels  28.8 us (92%)
  local copies, waits for them, and re-layouts  1.86 us (6%)
  between operations  0.65 us (2%)
    pallas_call x1, Pallas kernels, gathered(): pl.pallas_call(gather_kernel, out_shape=(jax.ShapeDtypeStruct((rows, widt...  28.8 us
    unnamed x4, local copies, waits for them, and re-layouts  1.86 us

profile of v5, /device:TPU:1, one launch (start us, length us, event | category | flops | bytes accessed | tf_op | source)
XLA Modules:
  0.0 31.3 jit_solution(12011052982875075594)
XLA Ops:
  0.6 0.0 copy-start
  0.6 0.6 %copy-done = s32[128]{0:T(128)S(1)} copy-done((s32[128]{0:T(128)S(1)}, s32[128]{0:T(128)}, u32[]{:S(2)}) %copy-start) | copy-done | bytes 536
  1.3 28.8 %shard_map.41 = (bf16[128,1024]{1,0:T(8,128)(2,1)S(1)}, f32[1,128]{1,0:T(1,128)S(1)}) custom-call(bf16[128,1024]{1,0:T(8,128)(2,1)} %emb_ref.1, s32[1,128]{1,0:T(1,128)S(1)} %bitcast.2), custom_call_target="tpu_custom_call" | custom-call | flops 1073741824 | bytes 524288 | tf_op jit(solution)/shard_map/pallas_call | solution.py:347
  30.1 0.7 %copy.6 = bf16[128,1024]{1,0:T(8,128)(2,1)} copy(bf16[128,1024]{1,0:T(8,128)(2,1)S(1)} %get-tuple-element.8) | data formatting | bytes 524288
  30.8 0.5 %copy.7 = f32[128]{0:T(128)} copy(f32[128]{0:T(128)S(1)} %bitcast.3) | data formatting | bytes 1024
Async XLA Ops:
  0.6 0.7 %copy-start = (s32[128]{0:T(128)S(1)}, s32[128]{0:T(128)}, u32[]{:S(2)}) copy-start(s32[128]{0:T(128)} %param.3) | copy-start | bytes 1540
